TPU v7x, 32 devices: a whole 2x2x4 slice. The times are simulated.
32 devices in a mesh: quarter: 4 (over y, x), row: 2 (over core), col: 4 (over z).
Axes of the slice: x: 2, y: 2, z: 4, core: 2. Of those that a mesh axis runs over, the one named last changes fastest.
Arguments:
- grad: bfloat16 [4, 4096, 4096], P('quarter', 'row', 'col'), may hold values from -6 to 6
- left_root: bfloat16 [4096, 4096], P('row', 'col'), may hold values from -1 to 3, as said below
- right_root: bfloat16 [4, 4096, 4096], P('quarter', 'row', 'col'), may hold values from -1 to 3, as said below
- momentum: float32 [4, 4096, 4096], P('quarter', 'row', 'col'), may hold values from -6 to 6
- weights: bfloat16 [4, 4096, 4096], P('quarter', 'row', 'col'), may hold values from -6 to 6
Outputs:
- momentum_new: float32 [4, 4096, 4096], P('quarter', 'row', 'col')
- new_weights: bfloat16 [4, 4096, 4096], P(None, ('row', 'quarter'), 'col')
Inputs may be any that keep to these rules, and one draw needn't show every extreme that they name: `left_root`: symmetric. `right_root`: each block symmetric.
All inputs are finite; a program needn't handle non-finite values.
Results may differ from a plain program's by a relative error of at most 0.001.
Values may be sent and summed in bfloat16 or wider, within the bound.
A program may use at most 128 MiB of HBM per device.

v0:
```python
import jax
import jax.numpy as jnp
from jax import lax
from jax.sharding import PartitionSpec as P

decay_rate = 0.9
step_rate = 0.1


def per_device(grad, left_root, right_root, momentum, weights):
    right_panel = lax.all_gather(right_root, "row", axis=1, tiled=True)[0]
    mixed = jnp.dot(
        lax.all_gather(grad, "col", axis=2, tiled=True)[0],
        right_panel,
        preferred_element_type=jnp.float32,
    ).astype(jnp.bfloat16)
    left_panel = lax.all_gather(left_root, "col", axis=1, tiled=True)
    product = jnp.dot(
        left_panel,
        lax.all_gather(mixed, "row", axis=0, tiled=True),
        preferred_element_type=jnp.float32,
    )
    renewed = decay_rate * momentum[0] + (1.0 - decay_rate) * product
    updated = (weights[0].astype(jnp.float32) - step_rate * renewed).astype(jnp.bfloat16)
    spread = lax.all_to_all(updated[None], "quarter", split_axis=1, concat_axis=0, tiled=True)
    return (renewed[None], spread)


def solution(mesh):
    placed = (
        P("quarter", "row", "col"),
        P("row", "col"),
        P("quarter", "row", "col"),
        P("quarter", "row", "col"),
        P("quarter", "row", "col"),
    )
    return jax.shard_map(
        per_device,
        mesh=mesh,
        in_specs=placed,
        out_specs=(P("quarter", "row", "col"), P(None, ("row", "quarter"), "col")),
        check_vma=False,
    )
```

profile of v0, /device:TPU:0, one launch (start us, length us, event | category | flops | bytes accessed | tf_op | source)
XLA Modules:
  0.0 786.2 jit_solution(6154761776581802596)
XLA Ops:
  7.2 0.0 all-gather.7.cloned.1.call-start
  7.2 0.7 all-gather.7.cloned.1.call-update
  7.9 0.0 all-gather.5.cloned.1.call-start
  7.9 0.7 all-gather.5.cloned.1.call-update
  8.6 0.0 all-gather.11.cloned.1.call-start
  8.7 0.7 all-gather.11.cloned.1.call-update
  9.4 0.0 all-gather.9.cloned.1.call-start
  9.4 22.7 %all-gather.7.cloned.1.call-done = bf16[1,4096,1024]{2,1,0:T(8,128)(2,1)} async-done(((bf16[1,2048,1024]{2,1,0:T(8,128)(2,1)}), bf16[1,4096,1024]{2,1,0:T(8,128)(2,1)}) %all-gather.7.cloned.1.call-update) | async-done | bytes 8388624 | tf_op jit(solution)/shard_map/all_gather | solution.py:11
  32.1 289.5 %all-gather.5.cloned.1.call-done = bf16[1,2048,4096]{2,1,0:T(8,128)(2,1)} async-done(((bf16[1,2048,1024]{2,1,0:T(8,128)(2,1)}), bf16[1,2048,4096]{2,1,0:T(8,128)(2,1)}) %all-gather.5.cloned.1.call-update) | async-done | bytes 16777232 | tf_op jit(solution)/shard_map/all_gather | solution.py:13
  321.7 23.6 %fusion.5 = bf16[2048,1024]{1,0:T(8,128)(2,1)} fusion(bf16[1,4096,1024]{2,1,0:T(8,128)(2,1)} %all-gather.7.cloned.1.call-done, bf16[1,2048,4096]{2,1,0:T(8,128)(2,1)} %all-gather.5.cloned.1.call-done), kind=kOutput, calls=%fused_computation.7 | convolution fusion | flops 17181966336 | bytes 29360128 | tf_op jit(solution)/shard_map/dot_general | solution.py:12
  345.3 0.0 all-gather.9.cloned.1.call-update
  345.3 9.2 %copy.15 = f32[1,2048,1024]{1,2,0:T(8,128)} copy(f32[1,2048,1024]{2,1,0:T(8,128)} %param.8) | data formatting | bytes 16777216 | tf_op args[3]
  354.5 6.5 copy.16
  361.0 247.3 %all-gather.11.cloned.1.call-done = bf16[2048,4096]{1,0:T(8,128)(2,1)} async-done(((bf16[2048,1024]{1,0:T(8,128)(2,1)}), bf16[2048,4096]{1,0:T(8,128)(2,1)}) %all-gather.11.cloned.1.call-update) | async-done | bytes 16777232 | tf_op jit(solution)/shard_map/all_gather | solution.py:17
  608.3 20.0 %all-gather.9.cloned.1.call-done = bf16[4096,1024]{1,0:T(8,128)(2,1)} async-done(((bf16[2048,1024]{1,0:T(8,128)(2,1)}), bf16[4096,1024]{1,0:T(8,128)(2,1)}) %all-gather.9.cloned.1.call-update) | async-done | bytes 8388624 | tf_op jit(solution)/shard_map/all_gather | solution.py:20
  628.3 0.0 copy-start.1
  628.3 23.8 %bitcast_add_fusion = f32[2048,1024]{0,1:T(8,128)S(1)} fusion(f32[1,2048,1024]{1,2,0:T(8,128)} %copy.15, bf16[4096,1024]{1,0:T(8,128)(2,1)} %all-gather.9.cloned.1.call-done, bf16[2048,4096]{1,0:T(8,128)(2,1)} %all-gather.11.cloned.1.call-done), kind=kOutput, calls=%fused_computation.4 | convolution fusion | flops 17186160640 | bytes 41943040 | tf_op jit(solution)/shard_map/dot_general | solution.py:18
  652.2 0.0 copy-start
  652.2 3.2 copy-done
  655.4 0.0 copy-done.1
  655.4 3.5 fusion.4
  658.9 20.3 %copy.17 = bf16[1,2048,1024]{2,0,1:T(2,128)(2,1)} copy(bf16[1,2048,1024]{1,2,0:T(8,128)(2,1)} %fusion.4) | data formatting | bytes 8388608 | tf_op jit(solution)/shard_map/broadcast_in_dim | solution.py:25
  679.1 0.6 broadcast.13
  679.7 26.2 %reduce = bf16[2048,1024]{1,0:T(8,128)(2,1)} reduce(bf16[2048,1,1024]{2,1,0:T(2,128)(2,1)} %bitcast.25, bf16[]{:T(256)} %broadcast.13), dimensions={1}, to_apply=%bitcast.21.reduce_sub_computation | reduce | bytes 8388610
  705.9 6.2 reshape.12
  712.1 4.9 all-to-all-start
  717.0 9.2 %copy.18 = f32[1,2048,1024]{2,1,0:T(8,128)} copy(f32[1,2048,1024]{1,2,0:T(8,128)} %bitcast.27) | data formatting | bytes 16777216
  726.3 38.8 %all-to-all-done = bf16[4,2,262144]{2,1,0:T(2,128)(2,1)} async-done(((bf16[4,2,262144]{2,1,0:T(2,128)(2,1)}), bf16[4,2,262144]{2,1,0:T(2,128)(2,1)}, u32[]{:S(2)}, u32[]{:S(2)}) %all-to-all-start) | async-done | bytes 4194336 | tf_op jit(solution)/shard_map/all_to_all | solution.py:25
  765.1 7.4 reshape.13
  772.5 7.1 copy.19
Async XLA Ops:
  7.2 25.0 %all-gather.7.cloned.1.call-start = ((), (), s32[]{:S(2)}) async-start(), calls=%async_computation.2 | async-start | bytes 12582912 | tf_op jit(solution)/shard_map/all_gather | solution.py:11
  7.9 313.8 %all-gather.5.cloned.1.call-start = ((), (), s32[]{:S(2)}) async-start(), calls=%async_computation.1 | async-start | bytes 20971520 | tf_op jit(solution)/shard_map/all_gather | solution.py:13
  8.6 599.6 %all-gather.11.cloned.1.call-start = ((), (), s32[]{:S(2)}) async-start(), calls=%async_computation.4 | async-start | bytes 20971520 | tf_op jit(solution)/shard_map/all_gather | solution.py:17
  9.4 618.9 %all-gather.9.cloned.1.call-start = ((), (), s32[]{:S(2)}) async-start(), calls=%async_computation.3 | async-start | bytes 12582912 | tf_op jit(solution)/shard_map/all_gather | solution.py:20
  628.3 27.1 %copy-start.1 = (bf16[1,2048,1024]{1,2,0:T(8,128)(2,1)S(1)}, bf16[1,2048,1024]{1,2,0:T(8,128)(2,1)}, u32[]{:S(2)}) copy-start(bf16[1,2048,1024]{1,2,0:T(8,128)(2,1)} %copy.16) | copy-start | bytes 12582916
  652.2 3.2 copy-start
  712.1 53.0 %all-to-all-start = ((bf16[4,2,262144]{2,1,0:T(2,128)(2,1)}), bf16[4,2,262144]{2,1,0:T(2,128)(2,1)}, u32[]{:S(2)}, u32[]{:S(2)}) async-start(bf16[4,2,262144]{2,1,0:T(2,128)(2,1)} %reshape.12), calls=%async_computation | async-start | bytes 8388608 | tf_op jit(solution)/shard_map/all_to_all | solution.py:25
Sparse Core Ops, SparseCore 0:
  9.5 22.5 all-gather.6
  33.7 287.9 all-gather.4
  323.2 284.9 all-gather.10
  610.2 18.0 all-gather.8
where the time goes:
time: 787 us; the launch traced here: 786 us
  waiting for transfers between devices  620 us (79%)
  local copies, waits for them, and re-layouts  69.7 us (9%)
  matrix products  47.5 us (6%)
  other arithmetic  29.7 us (4%)
  between operations  13.8 us (2%)
    all_gather x1, waiting for transfers between devices, per_device(): lax.all_gather(grad, 'col', axis=2, tiled=True)[0]  290 us
    all_gather x1, waiting for transfers between devices, per_device(): left_panel = lax.all_gather(left_root, 'col', axis=1, tiled=True)  247 us
    unnamed x11, local copies, waits for them, and re-layouts  49.4 us
    all_to_all x1, waiting for transfers between devices, per_device(): lax.all_to_all(updated[None], 'quarter', split_axis=1, concat_axis=0, til...  38.8 us
    unnamed x1, other arithmetic  26.2 us
    dot_general x1, matrix products, per_device(): jnp.dot(left_panel, lax.all_gather(mixed, 'row', axis=0, tiled=True), pre...  23.8 us
    dot_general x1, matrix products, per_device(): jnp.dot(lax.all_gather(grad, 'col', axis=2, tiled=True)[0], right_panel,...  23.6 us
    all_gather x1, waiting for transfers between devices, per_device(): right_panel = lax.all_gather(right_root, 'row', axis=1, tiled=True)[0]  22.7 us
  transfers between devices with their start and end apart: 5, of which 5 were waited for; matrix products, arithmetic and copies ran while one was open for 6% of the time, Pallas kernels for 0%

commit v1 on v0

--- a/solution.py
+++ b/solution.py
@@ -1,13 +1,363 @@
+import functools
+
 import jax
 import jax.numpy as jnp
 from jax import lax
+from jax.experimental import pallas as pl
+from jax.experimental.pallas import tpu as pltpu
 from jax.sharding import PartitionSpec as P
 
 decay_rate = 0.9
 step_rate = 0.1
 
-
-def per_device(grad, left_root, right_root, momentum, weights):
+CHUNKS = 8
+PARTS = 2
+
+
+def remote(src, dst, send, recv, device):
+    return pltpu.make_async_remote_copy(
+        src_ref=src, dst_ref=dst, send_sem=send, recv_sem=recv,
+        device_id=device, device_id_type=pl.DeviceIdType.MESH,
+    )
+
+
+def kernel(
+    grad, left, right, mom, wts, out_m, out_w,
+    lbuf, gbuf, rbuf, mix, stage, mslot,
+    lz_send, lz_recv, lxy_send, lxy_recv, local, own_send, own_recv,
+    near_send, near_recv, far_send, far_recv,
+    ms_send, ms_recv, me_send, me_recv,
+    a_send, a_recv, m_in, m_out,
+):
+    rows, cols = left.shape
+    lane = rows // 4
+    step = rows // CHUNKS
+    q, r, c = lax.axis_index("quarter"), lax.axis_index("row"), lax.axis_index("col")
+    peers = [3 - q, q + 1 - 2 * (q % 2), (q + 2) % 4]
+    twin = (q, 1 - r, c)
+    inner = (c + 1) // 2 % 2 == 1
+    outer = (c + 1) // 2 % 2 == 0
+    before, after = (q, r, c - 1), (q, r, c + 1)
+    low = c // 2 == 0
+    pair = c + 1 - 2 * (c % 2)
+    other = 3 - c
+    mine = pl.ds(pl.multiple_of(q * lane, lane), lane)
+
+    barrier = pltpu.get_barrier_semaphore()
+    for p in peers:
+        pl.semaphore_signal(barrier, inc=1, device_id=(p, r, c), device_id_type=pl.DeviceIdType.MESH)
+    pl.semaphore_signal(barrier, inc=1, device_id=twin, device_id_type=pl.DeviceIdType.MESH)
+
+    @pl.when(c > 0)
+    def _():
+        pl.semaphore_signal(barrier, inc=1, device_id=before, device_id_type=pl.DeviceIdType.MESH)
+
+    @pl.when(c < 3)
+    def _():
+        pl.semaphore_signal(barrier, inc=1, device_id=after, device_id_type=pl.DeviceIdType.MESH)
+
+    @pl.when(inner)
+    def _():
+        pl.semaphore_wait(barrier, 6)
+
+    @pl.when(outer)
+    def _():
+        pl.semaphore_wait(barrier, 5)
+
+    def lz(k, way, src):
+        return remote(src, lbuf.at[k, mine], lz_send.at[k * 2 + way], lz_recv.at[k], after if way else before)
+
+    def lxy(k, t):
+        piece = lbuf.at[k, mine]
+        return remote(piece, piece, lxy_send.at[k * 3 + t], lxy_recv.at[k * 4 + q], (peers[t], r, c))
+
+    @pl.when(c < 3)
+    def _():
+        lz(c, 1, left.at[mine]).start()
+
+    @pl.when(c > 0)
+    def _():
+        lz(c, 0, left.at[mine]).start()
+
+    copy_l = pltpu.make_async_copy(left, lbuf.at[c], local.at[0])
+    copy_l.start()
+
+    def g_own():
+        return remote(grad.at[0], gbuf.at[c], own_send.at[0], own_recv.at[0], (q, r, other))
+
+    def r_own():
+        half = rbuf.at[0, pl.ds(pl.multiple_of(r * rows, rows), rows)]
+        return remote(right.at[0], half, own_send.at[1], own_recv.at[1], twin)
+
+    def r_end():
+        half = rbuf.at[1, pl.ds(pl.multiple_of(r * rows, rows), rows)]
+        return remote(right.at[0], half, own_send.at[2], own_recv.at[2], (q, r, pair))
+
+    def r_twin():
+        half = rbuf.at[1, pl.ds(pl.multiple_of(r * rows, rows), rows)]
+        return remote(half, half, own_send.at[3], own_recv.at[3], twin)
+
+    copy_g = pltpu.make_async_copy(grad.at[0], gbuf.at[c], local.at[1])
+    copy_r = pltpu.make_async_copy(
+        right.at[0], rbuf.at[0, pl.ds(pl.multiple_of(r * rows, rows), rows)], local.at[2])
+
+    @pl.when(outer)
+    def _():
+        r_end().start()
+
+    @pl.when(inner)
+    def _():
+        copy_g.start()
+        copy_r.start()
+        r_own().start()
+
+    for d in (1, 2, 3):
+        @pl.when(c - d >= 0)
+        def _():
+            k = c - d
+            lz(k, 1, lbuf.at[k, mine]).wait_recv()
+
+            @pl.when(c < 3)
+            def _():
+                lz(k, 1, lbuf.at[k, mine]).start()
+            for t in range(3):
+                lxy(k, t).start()
+
+        @pl.when(c + d <= 3)
+        def _():
+            k = c + d
+            lz(k, 0, lbuf.at[k, mine]).wait_recv()
+
+            @pl.when(c > 0)
+            def _():
+                lz(k, 0, lbuf.at[k, mine]).start()
+            for t in range(3):
+                lxy(k, t).start()
+
+        if d == 1:
+            @pl.when(inner)
+            def _():
+                g_own().start()
+
+    def chunk(i):
+        return pl.ds(i * step if isinstance(i, int) else pl.multiple_of(i * step, step), step)
+
+    def deep(half, i):
+        return pl.ds(pl.multiple_of(half * rows + i * step, step), step)
+
+    def near(i):
+        return remote(grad.at[0, chunk(i)], gbuf.at[c, chunk(i)], near_send.at[i], near_recv.at[i], (q, r, pair))
+
+    def far(i):
+        part = gbuf.at[pair, chunk(i)]
+        return remote(part, part, far_send.at[i], far_recv.at[i], (q, r, other))
+
+    def mix_twin(i):
+        part = mix.at[deep(r, i)]
+        return remote(part, part, ms_send.at[i], ms_recv.at[i], twin)
+
+    def mix_end(i):
+        return remote(stage.at[i % 2], mix.at[deep(r, i)], me_send.at[i], me_recv.at[i], (q, r, pair))
+
+    @pl.when(outer)
+    def _():
+        r_end().wait_send()
+        for i in range(CHUNKS):
+            near(i).start()
+            if i >= 1:
+                near(i - 1).wait_send()
+        near(CHUNKS - 1).wait_send()
+        for i in range(CHUNKS):
+            mix_end(i).wait_recv()
+            mix_twin(i).start()
+
+    @pl.when(inner)
+    def _():
+        r_end().wait_recv()
+        r_twin().start()
+        near(0).wait_recv()
+        far(0).start()
+        copy_g.wait()
+        copy_r.wait()
+        r_own().wait_recv()
+        g_own().wait_recv()
+        r_twin().wait_recv()
+
+        def body(i, _):
+            @pl.when(i + 1 < CHUNKS)
+            def _():
+                near(i + 1).wait_recv()
+                far(i + 1).start()
+            far(i).wait_recv()
+
+            @pl.when(i >= 2)
+            def _():
+                mix_end(i - 2).wait_send()
+
+            def tile(n, _, which):
+                at = pl.ds(pl.multiple_of(n * 256, 256), 256)
+                total = jnp.zeros((step, 256), jnp.float32)
+                for k in range(4):
+                    total += jnp.dot(
+                        gbuf[k, chunk(i), :], rbuf[which, k * cols:(k + 1) * cols, at],
+                        preferred_element_type=jnp.float32)
+                if which:
+                    stage[i % 2, :, at] = total.astype(jnp.bfloat16)
+                else:
+                    mix[deep(r, i), at] = total.astype(jnp.bfloat16)
+                return 0
+
+            lax.fori_loop(0, cols // 256, functools.partial(tile, which=1), 0)
+            mix_end(i).start()
+            lax.fori_loop(0, cols // 256, functools.partial(tile, which=0), 0)
+            mix_twin(i).start()
+            return 0
+
+        lax.fori_loop(0, CHUNKS, body, 0)
+        mix_end(CHUNKS - 2).wait_send()
+        mix_end(CHUNKS - 1).wait_send()
+        for i in range(CHUNKS):
+            far(i).wait_send()
+        r_twin().wait_send()
+        r_own().wait_send()
+        g_own().wait_send()
+
+    copy_w = pltpu.make_async_copy(wts.at[0], rbuf.at[1, pl.ds(0, rows)], local.at[3])
+    copy_w.start()
+
+    order = [(p, h) for p in peers + [q] for h in range(PARTS)]
+    size = lane // PARTS
+
+    def strip(t):
+        p, h = order[t]
+        return pl.ds(pl.multiple_of(p * lane + h * size, size), size)
+
+    def m_load(t):
+        return pltpu.make_async_copy(mom.at[0, strip(t)], mslot.at[t % 4], m_in.at[t % 4])
+
+    def m_store(t):
+        return pltpu.make_async_copy(mslot.at[t % 4], out_m.at[0, strip(t)], m_out.at[t % 4])
+
+    def spread(t):
+        p, h = order[t]
+        target = out_w.at[q, pl.ds(h * size, size)]
+        source = rbuf.at[1, strip(t)]
+        if t // PARTS == 3:
+            return pltpu.make_async_copy(source, target, a_send.at[t])
+        return remote(source, target, a_send.at[t], a_recv.at[t], (p, r, c))
+
+    m_load(0).start()
+    m_load(1).start()
+    copy_l.wait()
+    for d in (1, 2, 3):
+        k = (c + d) % 4
+        for p in peers:
+            theirs = lbuf.at[k, pl.ds(pl.multiple_of(p * lane, lane), lane)]
+            remote(theirs, theirs, lxy_send.at[0], lxy_recv.at[k * 4 + p], twin).wait_recv()
+    for i in range(CHUNKS):
+        part = mix.at[deep(1 - r, i)]
+        remote(part, part, ms_send.at[i], ms_recv.at[i], twin).wait_recv()
+    copy_w.wait()
+
+    for t in range(4 * PARTS):
+        m_load(t).wait()
+
+        def tile(n, _):
+            at = pl.ds(pl.multiple_of(n * 256, 256), 256)
+            total = jnp.zeros((size, 256), jnp.float32)
+            for k in range(4):
+                total += jnp.dot(
+                    lbuf[k, strip(t), :], mix[k * cols:(k + 1) * cols, at],
+                    preferred_element_type=jnp.float32)
+            renewed = decay_rate * mslot[t % 4, :, at] + (1.0 - decay_rate) * total
+            mslot[t % 4, :, at] = renewed
+            old = rbuf[1, strip(t), at].astype(jnp.float32)
+            rbuf[1, strip(t), at] = (old - step_rate * renewed).astype(jnp.bfloat16)
+            return 0
+
+        lax.fori_loop(0, cols // 256, tile, 0)
+        m_store(t).start()
+        spread(t).start()
+        if t >= 2:
+            m_store(t - 2).wait()
+        if t + 2 < 4 * PARTS:
+            m_load(t + 2).start()
+
+    m_store(4 * PARTS - 2).wait()
+    m_store(4 * PARTS - 1).wait()
+
+    @pl.when(c < 3)
+    def _():
+        lz(c, 1, left.at[mine]).wait_send()
+
+    @pl.when(c > 0)
+    def _():
+        lz(c, 0, left.at[mine]).wait_send()
+
+    for d in (1, 2, 3):
+        @pl.when(c - d >= 0)
+        def _():
+            k = c - d
+
+            @pl.when(c < 3)
+            def _():
+                lz(k, 1, lbuf.at[k, mine]).wait_send()
+            for t in range(3):
+                lxy(k, t).wait_send()
+
+        @pl.when(c + d <= 3)
+        def _():
+            k = c + d
+
+            @pl.when(c > 0)
+            def _():
+                lz(k, 0, lbuf.at[k, mine]).wait_send()
+            for t in range(3):
+                lxy(k, t).wait_send()
+
+    for i in range(CHUNKS):
+        mix_twin(i).wait_send()
+    for t in range(3 * PARTS):
+        p, h = order[t]
+        spread(t).wait_send()
+        theirs = out_w.at[p, pl.ds(h * size, size)]
+        remote(theirs, theirs, a_send.at[t], a_recv.at[t], (p, r, c)).wait_recv()
+    for t in range(3 * PARTS, 4 * PARTS):
+        spread(t).wait()
+
+
+def one_kernel(grad, left_root, right_root, momentum, weights):
+    rows, cols = left_root.shape
+    bf16, dma = jnp.bfloat16, pltpu.SemaphoreType.DMA
+    anywhere = pl.BlockSpec(memory_space=pl.ANY)
+    return pl.pallas_call(
+        kernel,
+        out_shape=(
+            jax.ShapeDtypeStruct((1, rows, cols), jnp.float32),
+            jax.ShapeDtypeStruct((4, rows // 4, cols), bf16),
+        ),
+        in_specs=[anywhere] * 5,
+        out_specs=(anywhere, anywhere),
+        scratch_shapes=[
+            pltpu.VMEM((4, rows, cols), bf16),
+            pltpu.VMEM((4, rows, cols), bf16),
+            pltpu.VMEM((2, 2 * rows, cols), bf16),
+            pltpu.VMEM((2 * rows, cols), bf16),
+            pltpu.VMEM((2, rows // CHUNKS, cols), bf16),
+            pltpu.VMEM((4, rows // 4 // PARTS, cols), jnp.float32),
+            dma((8,)), dma((4,)), dma((12,)), dma((16,)), dma((4,)), dma((4,)), dma((4,)),
+            dma((CHUNKS,)), dma((CHUNKS,)), dma((CHUNKS,)), dma((CHUNKS,)),
+            dma((CHUNKS,)), dma((CHUNKS,)), dma((CHUNKS,)), dma((CHUNKS,)),
+            dma((4 * PARTS,)), dma((4 * PARTS,)), dma((4,)), dma((4,)),
+        ],
+        compiler_params=pltpu.CompilerParams(
+            collective_id=0, has_side_effects=True, vmem_limit_bytes=63 * 1024 * 1024),
+        cost_estimate=pl.CostEstimate(
+            flops=4 * 4 * rows * rows * cols, bytes_accessed=36 * rows * cols, transcendentals=0),
+    )(grad, left_root, right_root, momentum, weights)
+
+
+def by_collectives(grad, left_root, right_root, momentum, weights):
     right_panel = lax.all_gather(right_root, "row", axis=1, tiled=True)[0]
     mixed = jnp.dot(
         lax.all_gather(grad, "col", axis=2, tiled=True)[0],
@@ -34,8 +384,10 @@
         P("quarter", "row", "col"),
         P("quarter", "row", "col"),
     )
+    shape = mesh.shape
+    lines = (shape["quarter"], shape["row"], shape["col"]) == (4, 2, 4)
     return jax.shard_map(
-        per_device,
+        one_kernel if lines else by_collectives,
         mesh=mesh,
         in_specs=placed,
         out_specs=(P("quarter", "row", "col"), P(None, ("row", "quarter"), "col")),

time: 787 us -> 312 us (0.40)
  waiting for transfers between devices: 620 us -> 0 us
  Pallas kernels: 0 us -> 301 us
  local copies, waits for them, and re-layouts: 69.7 us -> 10.6 us
  matrix products: 47.5 us -> 0 us
  other arithmetic: 29.7 us -> 0 us
  between operations: 13.8 us -> 0.65 us
    all_gather x4 -> x0, waiting for transfers between devices: 580 us -> none  [the longest x1 290 us: per_device(): lax.all_gather(grad, 'col', axis=2, tiled=True)[0]]
    pallas_call x0 -> x1, Pallas kernels: none -> 301 us  [one_kernel(): pl.pallas_call(kernel, out_shape=(jax.ShapeDtypeStruct((1, rows, cols), j...]
    dot_general x2 -> x0, matrix products: 47.5 us -> none  [the longest x1 23.8 us: per_device(): jnp.dot(left_panel, lax.all_gather(mixed, 'row', axis=0, tiled=True), pre...]
    unnamed x11 -> x4, local copies, waits for them, and re-layouts: 49.4 us -> 10.6 us
    all_to_all x1 -> x0, waiting for transfers between devices: 38.8 us -> none  [per_device(): lax.all_to_all(updated[None], 'quarter', split_axis=1, concat_axis=0, til...]
    unnamed x1 -> x0, other arithmetic: 26.2 us -> none
    broadcast_in_dim x1 -> x0, local copies, waits for them, and re-layouts: 20.3 us -> none  [per_device(): updated[None]]
  transfers between devices with their start and end apart: 5 -> 0, of which waited for: 5 -> 0; matrix products, arithmetic and copies ran while one was open for 6% -> 0% of each run, Pallas kernels for 0% -> 0%
where the time goes in v1:
time: 312 us
  Pallas kernels  301 us (96%)
  local copies, waits for them, and re-layouts  10.6 us (3%)
    pallas_call x1, Pallas kernels, one_kernel(): pl.pallas_call(kernel, out_shape=(jax.ShapeDtypeStruct((1, rows, cols), j...  301 us
    unnamed x4, local copies, waits for them, and re-layouts  10.6 us

profile of v1, /device:TPU:0, one launch (start us, length us, event | category | flops | bytes accessed | tf_op | source)
XLA Modules:
  0.0 311.9 jit_solution(10949169277905014437)
XLA Ops:
  0.6 300.6 %shard_map.68 = (f32[1,2048,1024]{2,1,0:T(8,128)}, bf16[4,512,1024]{2,1,0:T(8,128)(2,1)}) custom-call(bf16[1,2048,1024]{2,1,0:T(8,128)(2,1)} %grad.1, bf16[2048,1024]{1,0:T(8,128)(2,1)} %left.1, bf16[1,2048,1024]{2,1,0:T(8,128)(2,1)} %right.1, f32[1,2048,1024]{2,1,0:T(8,128)} %mom.1, bf16[1,2048,1024]{2,1,0:T(8,128)(2,1)} %wts.1), custom_call_target="tpu_custom_call" | custom-call | flops 68719476736 | bytes 75497472 | tf_op jit(solution)/shard_map/pallas_call | solution.py:333
  301.2 0.0 copy-start
  301.3 8.6 %copy.9 = f32[1,2048,1024]{2,1,0:T(8,128)} copy(f32[1,2048,1024]{2,1,0:T(8,128)} %get-tuple-element.4) | data formatting | bytes 16777216
  309.9 0.0 copy-done
  309.9 2.0 copy.10
Async XLA Ops:
  301.2 8.6 %copy-start = (bf16[4,512,1024]{2,1,0:T(8,128)(2,1)S(1)}, bf16[4,512,1024]{2,1,0:T(8,128)(2,1)}, u32[]{:S(2)}) copy-start(bf16[4,512,1024]{2,1,0:T(8,128)(2,1)} %get-tuple-element.5) | copy-start | bytes 12582916

commit v2 on v1

--- a/solution.py
+++ b/solution.py
@@ -103,6 +103,13 @@
 
     @pl.when(outer)
     def _():
+        @pl.when(c == 0)
+        def _():
+            lz(c, 1, left.at[mine]).wait_send()
+
+        @pl.when(c == 3)
+        def _():
+            lz(c, 0, left.at[mine]).wait_send()
         r_end().start()
 
     @pl.when(inner)
@@ -134,7 +141,7 @@
             for t in range(3):
                 lxy(k, t).start()
 
-        if d == 1:
+        if d == 2:
             @pl.when(inner)
             def _():
                 g_own().start()
@@ -286,12 +293,9 @@
     m_store(4 * PARTS - 2).wait()
     m_store(4 * PARTS - 1).wait()
 
-    @pl.when(c < 3)
+    @pl.when(inner)
     def _():
         lz(c, 1, left.at[mine]).wait_send()
-
-    @pl.when(c > 0)
-    def _():
         lz(c, 0, left.at[mine]).wait_send()
 
     for d in (1, 2, 3):

time: 312 us -> 313 us (level)
  no operation moved by 1% of the time
where the time goes in v2:
time: 313 us
  Pallas kernels  301 us (96%)
  local copies, waits for them, and re-layouts  10.6 us (3%)
    pallas_call x1, Pallas kernels, one_kernel(): pl.pallas_call(kernel, out_shape=(jax.ShapeDtypeStruct((1, rows, cols), j...  301 us
    unnamed x4, local copies, waits for them, and re-layouts  10.6 us

profile of v2, /device:TPU:0, one launch (start us, length us, event | category | flops | bytes accessed | tf_op | source)
XLA Modules:
  0.0 312.6 jit_solution(1662201333322268469)
XLA Ops:
  0.6 301.3 %shard_map.68 = (f32[1,2048,1024]{2,1,0:T(8,128)}, bf16[4,512,1024]{2,1,0:T(8,128)(2,1)}) custom-call(bf16[1,2048,1024]{2,1,0:T(8,128)(2,1)} %grad.1, bf16[2048,1024]{1,0:T(8,128)(2,1)} %left.1, bf16[1,2048,1024]{2,1,0:T(8,128)(2,1)} %right.1, f32[1,2048,1024]{2,1,0:T(8,128)} %mom.1, bf16[1,2048,1024]{2,1,0:T(8,128)(2,1)} %wts.1), custom_call_target="tpu_custom_call" | custom-call | flops 68719476736 | bytes 75497472 | tf_op jit(solution)/shard_map/pallas_call | solution.py:337
  301.9 0.0 copy-start
  302.0 8.6 %copy.9 = f32[1,2048,1024]{2,1,0:T(8,128)} copy(f32[1,2048,1024]{2,1,0:T(8,128)} %get-tuple-element.4) | data formatting | bytes 16777216
  310.6 0.0 copy-done
  310.6 2.0 copy.10
Async XLA Ops:
  301.9 8.6 %copy-start = (bf16[4,512,1024]{2,1,0:T(8,128)(2,1)S(1)}, bf16[4,512,1024]{2,1,0:T(8,128)(2,1)}, u32[]{:S(2)}) copy-start(bf16[4,512,1024]{2,1,0:T(8,128)(2,1)} %get-tuple-element.5) | copy-start | bytes 12582916
